TPU v7x, 512 devices: a whole 4x4x16 slice. The times are simulated.
512 devices in a mesh: outer: 32 (over y, z_lo), rep: 16 (over z_hi, x, core).
Axes of the slice: x: 4, y: 4, z: 16 (z_hi: 2, z_lo: 8; z = z_hi * 8 + z_lo), core: 2. Of those that a mesh axis runs over, the one named last changes fastest.
Arguments:
- activations: bfloat16 [16, 6144, 4096], P('rep', 'outer'), may hold values from -6 to 6
- out_grads: bfloat16 [16, 4096, 1024], P('rep', 'outer'), may hold values from -0.25 to 0.25
- error_buffer: float32 [16, 6144, 1024], P('rep', 'outer'), may hold values from -6 to 6
- right_factor: float32 [64, 1024], replicated, may hold values from -0.1875 to 0.1875
Outputs:
- update: bfloat16 [1024, 6144], P('rep')
- new_error: float32 [16, 6144, 1024], P('rep', 'outer')
- new_factor: float32 [64, 1024], replicated
All inputs are finite; a program needn't handle non-finite values.
Results may differ from a plain program's by a relative error of at most 0.001.
Values may be sent and summed in bfloat16 or wider, within the bound.
A program may use at most 64 MiB of HBM per device.

v0:
```python
import jax
import jax.numpy as jnp
from jax import lax
from jax.sharding import PartitionSpec as P


def shifted_lower(gram):
    width = gram.shape[0]
    shift = 0.0001 * jnp.trace(gram) / width
    return jnp.linalg.cholesky(gram + shift * jnp.eye(width, dtype=gram.dtype))


def body(activations, out_grads, error_buffer, right_factor):
    replicas = lax.axis_size("rep")
    inputs = activations[0]
    cotangents = out_grads[0]
    summed = jnp.dot(
        inputs,
        lax.all_gather(cotangents, "outer", axis=0, tiled=True),
        preferred_element_type=jnp.float32,
    )
    corrected = summed + error_buffer[0]
    left_part = jnp.dot(corrected, right_factor.T, precision=lax.Precision.HIGHEST)
    p_raw = lax.psum(left_part, "rep") / replicas
    gram_part = jnp.dot(p_raw.T, p_raw, precision=lax.Precision.HIGHEST)
    gram = lax.psum(gram_part, "outer")
    lower = shifted_lower(gram)
    p_orth = jax.scipy.linalg.solve_triangular(lower, p_raw.T, lower=True).T
    right_part = jnp.dot(p_orth.T, corrected, precision=lax.Precision.HIGHEST)
    new_factor = lax.psum(right_part, ("outer", "rep")) / replicas
    approx = jnp.dot(p_orth, new_factor, precision=lax.Precision.HIGHEST)
    new_error = (corrected - approx)[None]
    columns = new_factor.shape[1] // replicas
    first = lax.axis_index("rep") * columns
    own_block = lax.dynamic_slice_in_dim(approx, first, columns, 1).T.astype(jnp.bfloat16)
    update = lax.all_gather(own_block, "outer", axis=1, tiled=True)
    return (update, new_error, new_factor)


def solution(mesh):
    placed = (P("rep", "outer", None), P("rep", "outer", None), P("rep", "outer", None), P())
    return jax.shard_map(
        body,
        mesh=mesh,
        in_specs=placed,
        out_specs=(P("rep", None), P("rep", "outer", None), P()),
        check_vma=False,
    )
```

profile of v0, /device:TPU:1, one launch (start us, length us, event | category | flops | bytes accessed | tf_op | source)
XLA Modules:
  0.0 1222.3 jit_solution(3908515004919042147)
XLA Ops:
  7.2 0.0 copy-start
  7.2 0.0 all-gather.4.cloned.1.call-start
  7.2 0.7 all-gather.4.cloned.1.call-update
  7.9 0.0 copy-start.2
  7.9 0.0 all-reduce.2.cloned.1.call-start
  8.0 245.7 %all-gather.4.cloned.1.call-done = bf16[1,4096,1024]{2,1,0:T(8,128)(2,1)} async-done(((bf16[1,128,1024]{2,1,0:T(8,128)(2,1)}), bf16[1,4096,1024]{2,1,0:T(8,128)(2,1)}) %all-gather.4.cloned.1.call-update) | async-done | bytes 8388624 | tf_op jit(solution)/shard_map/all_gather | solution.py:19
  253.7 0.0 copy-done
  253.7 5.3 fusion.3
  259.0 0.0 copy-done.2
  259.0 0.9 fusion.20
  259.9 129.4 %psum.21 = f32[192,64]{0,1:T(8,128)S(1)} all-reduce(f32[192,64]{0,1:T(8,128)S(1)} %fusion.20), channel_id=1, replica_groups=mesh['outer'=32,'rep'=16] {'rep'}, use_global_device_ids=true, to_apply=%region_0.0 | all-reduce | flops 12288 | bytes 98304 | tf_op jit(solution)/shard_map/psum | solution.py:24
  389.3 0.2 fusion.10
  389.5 204.9 %psum.22 = f32[64,64]{1,0:T(8,128)S(1)} all-reduce(f32[64,64]{1,0:T(8,128)S(1)} %fusion.10), channel_id=1, replica_groups=mesh['outer'=32,'rep'=16] {'outer'}, use_global_device_ids=true, to_apply=%region_1.0 | all-reduce | flops 4096 | bytes 32768 | tf_op jit(solution)/shard_map/psum | solution.py:26
  594.4 0.6 select_reduce_fusion.1
  595.7 0.1 copy.11
  595.8 5.8 cholesky.17
  601.7 0.6 compare_reduce_fusion
  602.3 0.7 fusion.13
  603.0 4.9 custom-call.7
  607.9 0.3 fusion.8
  608.2 1.3 fusion.21
  609.5 0.0 all-reduce.2.cloned.1.call-update
  609.5 484.9 %all-reduce.2.cloned.1.call-done = f32[64,1024]{1,0:T(8,128)} async-done(((f32[64,1024]{1,0:T(8,128)}), f32[64,1024]{1,0:T(8,128)}) %all-reduce.2.cloned.1.call-update) | async-done | bytes 262160 | tf_op jit(solution)/shard_map/psum | solution.py:30
  1094.4 1.0 broadcast_multiply_fusion
  1095.4 0.0 copy-start.1
  1095.4 0.8 fusion.22
  1096.2 1.0 subtract_bitcast_fusion
  1097.2 0.1 fusion.12
  1097.3 0.1 copy.12
  1097.4 115.5 %all-gather.1 = bf16[32,192,64]{1,2,0:T(8,128)(2,1)S(1)} all-gather(bf16[1,192,64]{1,2,0:T(8,128)(2,1)S(1)} %copy.12), channel_id=1, replica_groups=mesh['outer'=32,'rep'=16] {'outer'}, dimensions={0}, use_global_device_ids=true | all-gather | bytes 811008 | tf_op jit(solution)/shard_map/all_gather | solution.py:36
  1212.9 0.6 copy.13
  1213.4 2.0 reshape.18
  1215.5 0.0 copy-done.1
  (3 shorter events, 0.1 us)
Async XLA Ops:
  7.2 246.5 %copy-start = (bf16[1,192,4096]{2,1,0:T(8,128)(2,1)S(1)}, bf16[1,192,4096]{2,1,0:T(8,128)(2,1)}, u32[]{:S(2)}) copy-start(bf16[1,192,4096]{2,1,0:T(8,128)(2,1)} %param.4) | copy-start | bytes 4718596
  7.2 246.5 %all-gather.4.cloned.1.call-start = ((), (), s32[]{:S(2)}) async-start(), calls=%async_computation.1 | async-start | bytes 8650752 | tf_op jit(solution)/shard_map/all_gather | solution.py:19
  7.9 251.1 %copy-start.2 = (f32[64,1024]{1,0:T(8,128)S(1)}, f32[64,1024]{1,0:T(8,128)}, u32[]{:S(2)}) copy-start(f32[64,1024]{1,0:T(8,128)} %param.7) | copy-start | bytes 786436
  7.9 1086.5 %all-reduce.2.cloned.1.call-start = ((), (), s32[]{:S(2)}) async-start(), calls=%async_computation | async-start | bytes 524288 | tf_op jit(solution)/shard_map/psum | solution.py:30
  1095.4 120.1 %copy-start.1 = (f32[64,1024]{1,0:T(8,128)}, f32[64,1024]{1,0:T(8,128)S(1)}, u32[]{:S(2)}) copy-start(f32[64,1024]{1,0:T(8,128)S(1)} %broadcast_multiply_fusion) | copy-start | bytes 786436
Sparse Core Ops, SparseCore 0:
  10.1 243.5 all-gather.3
  609.6 484.7 all-reduce.1
where the time goes:
time: 1230 us; the launch traced here: 1220 us
  waiting for transfers between devices  731 us (59%)
  blocking collectives  450 us (37%)
  between operations  14.8 us (1%)
  other arithmetic  14.6 us (1%)
    psum x1, waiting for transfers between devices, body(): new_factor = lax.psum(right_part, ('outer', 'rep')) / replicas  485 us
    all_gather x1, waiting for transfers between devices, body(): lax.all_gather(cotangents, 'outer', axis=0, tiled=True)  246 us
    psum x1, blocking collectives, body(): gram = lax.psum(gram_part, 'outer')  205 us
    psum x1, blocking collectives, body(): p_raw = lax.psum(left_part, 'rep') / replicas  129 us
    all_gather x1, blocking collectives, body(): update = lax.all_gather(own_block, 'outer', axis=1, tiled=True)  115 us
  transfers between devices with their start and end apart: 2, of which 2 were waited for; matrix products, arithmetic and copies ran while one was open for 0% of the time, Pallas kernels for 0%

commit v1 on v0

v1 whole, which is shorter than its diff:
```python
import functools

import jax
import jax.numpy as jnp
from jax import lax
from jax.experimental import pallas as pl
from jax.experimental.pallas import tpu as pltpu
from jax.sharding import PartitionSpec as P

HI = lax.Precision.HIGHEST
F32 = jnp.float32


def dot(a, b, ca, cb, precision=None):
    return lax.dot_general(
        a, b, (((ca,), (cb,)), ((), ())), precision=precision, preferred_element_type=F32
    )


def copy_to(src, dst, send, recv, outer, rep):
    return pltpu.make_async_remote_copy(
        src_ref=src,
        dst_ref=dst,
        send_sem=send,
        recv_sem=recv,
        device_id={"outer": outer, "rep": rep},
        device_id_type=pl.DeviceIdType.MESH,
    )


class Round:
    def __init__(self, n, me, place, src, dst, send, recv, first):
        self.out, self.into = [], []
        for k in range(1, n):
            to, frm = lax.rem(me + k, n), lax.rem(me + n - k, n)
            s, r = send.at[first + k - 1], recv.at[first + k - 1]
            self.out.append(copy_to(src(to), dst(me), s, r, *place(to)))
            self.into.append(copy_to(src(to), dst(frm), s, r, *place(to)))

    def start(self):
        for c in self.out:
            c.start()

    def wait(self):
        for c in self.into:
            c.wait_recv()

    def drain(self):
        for c in self.out:
            c.wait_send()


def kernel(
    ny, nz, nh, replicas,
    a_ref, g_ref, e_ref, r_ref,
    update_ref, error_ref, factor_ref,
    g_all, corr, p_part, p_rs, p_h, p_all8,
    pt_all, gram_y, gram_z1, gram_z2, gram_all,
    m_part, m_rs, m_y_src, m_y, m_z1, m_z2, m_agy, m_all,
    z_send, z_recv, yp_send, yp_recv, ym_send, ym_recv,
    rp_send, rp_recv, rm_send, rm_recv, send, recv,
):
    ng = replicas // nh
    zq = nz // 2
    blocks = ny * nz
    tok, width = g_ref.shape
    rank = r_ref.shape[0]
    rows = a_ref.shape[0]
    outer, rep = lax.axis_index("outer"), lax.axis_index("rep")
    y, z = outer // nz, outer % nz
    h, g = rep // ng, rep % ng
    core = rep % 2
    zlow, zhalf = z % zq, z // zq
    y_up, y_down, y_far = (y + 1) % ny, (y + ny - 1) % ny, (y + 2) % ny
    h_other = (h + 1) % nh

    barrier = pltpu.get_barrier_semaphore()
    peers = [((y + k) % ny * nz + z, rep) for k in range(1, ny)]
    peers += [(y * nz + (z + k) % nz, rep) for k in range(1, nz)]
    peers += [(outer, h * ng + (g + k) % ng) for k in range(1, ng)]
    peers += [(outer, h_other * ng + g), (y * nz + (z + zq) % nz, h_other * ng + g)]
    for o, r in peers:
        pl.semaphore_signal(
            barrier, inc=1, device_id={"outer": o, "rep": r},
            device_id_type=pl.DeviceIdType.MESH,
        )
    g_all[outer] = g_ref[...]
    corr[...] = e_ref[...]
    pl.semaphore_wait(barrier, len(peers))

    half = tok // 2
    step_n = min(256, width)

    def multiply(block):
        a = a_ref[:, pl.ds(pl.multiple_of(block * tok, tok), tok)]
        for n in range(0, width, step_n):
            corr[:, n : n + step_n] += dot(a, g_all[block, :, n : n + step_n], 1, 0)

    def place_of(q):
        d = (q + 1) // 2
        return z + d * (1 - 2 * (q % 2))

    def z_copy(zb, q, to):
        slot = g_all.at[y * nz + zb]
        return copy_to(slot, slot, z_send.at[q], z_recv.at[q], y * nz + to, rep)

    def yp_copy(yb, zb, q):
        slot = g_all.at[yb * nz + zb]
        return copy_to(slot, slot, yp_send.at[q], yp_recv.at[q], y_up * nz + z, rep)

    def ym_copy(yb, zb, q):
        slot = g_all.at[yb * nz + zb]
        return copy_to(slot, slot, ym_send.at[q], ym_recv.at[q], y_down * nz + z, rep)

    def rp_copy(yb, zb, q):
        slot = g_all.at[yb * nz + zb, pl.ds(0, half)]
        return copy_to(slot, slot, rp_send.at[q], rp_recv.at[q], y_up * nz + z, rep)

    def rm_copy(yb, zb, q):
        slot = g_all.at[yb * nz + zb, pl.ds(half, half)]
        return copy_to(slot, slot, rm_send.at[q], rm_recv.at[q], y_down * nz + z, rep)

    def inside(zb):
        return jnp.logical_and(zb >= 0, zb < nz)

    for q, to in ((1, z + 1), (2, z - 1)):

        @pl.when(inside(to))
        def _():
            z_copy(z, q, to).start()

    yp_copy(y, z, 0).start()
    ym_copy(y, z, 0).start()
    multiply(outer)
    last = 2 * nz - 1

    def z_step(q, carry):
        zb = place_of(q)

        @pl.when(inside(zb))
        def _():
            z_copy(zb, q, (z + 1) % nz).wait_recv()
            to = z + 2 * (q % 2) - 1

            @pl.when(inside(to))
            def _():
                z_copy(zb, q + 2, to).start()

            yp_copy(y, zb, q).start()
            ym_copy(y, zb, q).start()
            multiply(y * nz + zb)

        return carry

    lax.fori_loop(1, last, z_step, 0)

    def y_step(q, carry):
        zb = place_of(q)

        @pl.when(inside(zb))
        def _():
            yp_copy(y_down, zb, q).wait_recv()
            rp_copy(y_down, zb, q).start()
            ym_copy(y_up, zb, q).wait_recv()
            rm_copy(y_up, zb, q).start()
            multiply(y_down * nz + zb)
            multiply(y_up * nz + zb)

        return carry

    lax.fori_loop(0, last, y_step, 0)

    def far_step(q, carry):
        zb = place_of(q)

        @pl.when(inside(zb))
        def _():
            rp_copy(y_far, zb, q).wait_recv()
            rm_copy(y_far, zb, q).wait_recv()
            multiply(y_far * nz + zb)

        return carry

    lax.fori_loop(0, last, far_step, 0)

    rows8 = rows // ng
    part = dot(corr[...], r_ref[...], 1, 1, HI) * (1.0 / replicas)
    p_part[...] = part.reshape(ng, rows8, rank)
    group = lambda j: (outer, h * ng + j)
    count = [0]

    def make(n, me, place, src, dst):
        first = count[0]
        count[0] += n - 1
        return Round(n, me, place, src, dst, send, recv, first)

    rounds = []

    def go(*args):
        r = make(*args)
        rounds.append(r)
        r.start()
        return r

    def total(ref, n):
        s = ref[0]
        for i in range(1, n):
            s = s + ref[i]
        return s

    rnd = go(ng, g, group, lambda j: p_part.at[j], lambda i: p_rs.at[i])
    p_rs[g] = p_part[g]
    rnd.wait()
    p_h[h] = total(p_rs, ng)
    if nh > 1:
        rnd = go(nh, h, lambda j: (outer, j * ng + g), lambda j: p_h.at[h], lambda i: p_h.at[i])
        rnd.wait()
    p_all8[g] = total(p_h, nh)
    rnd = go(ng, g, group, lambda j: p_all8.at[g], lambda i: p_all8.at[i])
    rnd.wait()
    p = p_all8[...].reshape(rows, rank)

    r8 = rank // ng
    pt = p.T
    gram_all[...] = dot(pt, pt, 1, 1, HI).reshape(ng, r8, rank)
    gram_y[y] = gram_all[g]
    in_y = lambda j: (j * nz + z, rep)
    in_z1 = lambda j: (y * nz + zhalf * zq + j, rep)
    gram_1 = go(ny, y, in_y, lambda j: gram_y.at[y], lambda i: gram_y.at[i])

    hr = rank // 2
    slot = y * nz + zlow * 2 + zhalf
    pt_all[core, slot] = jnp.where(core == 0, pt[:hr], pt[hr:])
    pt_1 = go(
        2, zhalf, lambda j: (y * nz + j * zq + zlow, rep),
        lambda j: pt_all.at[core, slot],
        lambda i: pt_all.at[core, y * nz + zlow * 2 + i],
    )

    mine = dot(pt, corr[...], 1, 0, HI)
    m_part[...] = mine.reshape(ng, r8, width)
    m_1 = go(ng, g, group, lambda j: m_part.at[j], lambda i: m_rs.at[i])
    m_rs[g] = m_part[g]

    gram_1.wait()
    gram_z1[zlow] = total(gram_y, ny)
    gram_2 = go(zq, zlow, in_z1, lambda j: gram_z1.at[zlow], lambda i: gram_z1.at[i])
    pt_1.wait()
    pair = lambda i: pt_all.at[core, pl.ds(y * nz + i * 2, 2)]
    pt_2 = go(zq, zlow, in_z1, lambda j: pair(zlow), pair)

    m_1.wait()
    wy = width // ny
    s = total(m_rs, ng)
    for i in range(ny):
        m_y_src[i] = s[:, i * wy : (i + 1) * wy]
    m_2 = go(ny, y, in_y, lambda j: m_y_src.at[j], lambda i: m_y.at[i])
    m_y[y] = m_y_src[y]

    gram_2.wait()
    gram_z2[zhalf] = total(gram_z1, zq)
    gram_3 = go(
        2, zhalf, lambda j: (y * nz + j * zq + zlow, rep),
        lambda j: gram_z2.at[zhalf], lambda i: gram_z2.at[i],
    )
    m_2.wait()
    m_z1[zlow] = total(m_y, ny)
    m_3 = go(zq, zlow, in_z1, lambda j: m_z1.at[zlow], lambda i: m_z1.at[i])
    pt_2.wait()
    column = lambda i: pt_all.at[core, pl.ds(i * nz, nz)]
    pt_3 = go(ny, y, in_y, lambda j: column(y), column)

    gram_3.wait()
    gram_all[g] = total(gram_z2, 2)
    gram_4 = go(ng, g, group, lambda j: gram_all.at[g], lambda i: gram_all.at[i])
    m_3.wait()
    w = h * 2 + zhalf
    m_z2[w] = total(m_z1, zq)
    m_4 = go(
        2 * nh, w, lambda j: (y * nz + j % 2 * zq + zlow, j // 2 * ng + g),
        lambda j: m_z2.at[w], lambda i: m_z2.at[i],
    )

    gram_4.wait()
    gram = gram_all[...].reshape(rank, rank)
    ri = lax.broadcasted_iota(jnp.int32, (rank, rank), 0)
    ci = lax.broadcasted_iota(jnp.int32, (rank, rank), 1)
    eye = (ri == ci).astype(F32)
    gram = gram + (0.0001 / rank) * jnp.sum(gram * eye) * eye
    full = jnp.concatenate([gram, eye], axis=1)
    x = [full[i : i + 8] for i in range(0, rank, 8)]
    sub = lax.broadcasted_iota(jnp.int32, (8, 1), 0)

    def eliminate(x, lo, hi):
        x = list(x)
        for j in range(lo, hi):
            b, i = divmod(j, 8)
            row = x[b][i : i + 1]
            scaled = row / row[:, j : j + 1]
            for k in range(b, len(x)):
                col = x[k][:, j : j + 1]
                if k == b:
                    col = jnp.where(sub > i, col, 0.0)
                x[k] = x[k] - col * scaled
        return x

    third = rank // 3
    x = eliminate(x, 0, third)

    m_4.wait()
    m_agy[y] = total(m_z2, 2 * nh) * (1.0 / replicas)
    m_5 = go(ny, y, in_y, lambda j: m_agy.at[y], lambda i: m_agy.at[i])
    pt_3.wait()
    side = lambda i: pt_all.at[i]
    pt_4 = go(2, core, lambda j: (outer, rep // 2 * 2 + j), lambda j: side(core), side)
    x = eliminate(x, third, 2 * third)
    m_5.wait()
    m_all[g] = jnp.concatenate([m_agy[i] for i in range(ny)], axis=1)
    m_6 = go(ng, g, group, lambda j: m_all.at[g], lambda i: m_all.at[i])
    x = eliminate(x, 2 * third, rank)
    full = jnp.concatenate(x, axis=0)
    pivots = jnp.sum(full[:, :rank] * eye, axis=1, keepdims=True)
    inverse = full[:, rank:] * (1.0 / jnp.sqrt(pivots))
    p_orth = dot(p, inverse, 1, 1, HI)

    m_6.wait()
    factor = dot(inverse, m_all[...].reshape(rank, width), 1, 0, HI)
    factor_ref[...] = factor
    for n in range(0, width, step_n):
        error_ref[:, n : n + step_n] = corr[:, n : n + step_n] - dot(
            p_orth, factor[:, n : n + step_n], 1, 0, HI
        )
    columns = width // replicas
    both = factor_ref[:, pl.ds(pl.multiple_of(rep // 2 * (2 * columns), 2 * columns), 2 * columns)]
    own = jnp.where(core == 0, both[:, :columns], both[:, columns:])
    weights = dot(own, inverse, 0, 0, HI)
    pt_4.wait()

    def spread(i, carry):
        yb, zb = i // (nz // 2), i % (nz // 2) * 2

        def decompressed(zb):
            at = yb * nz + zb % zq * 2 + zb // zq
            block = jnp.concatenate([pt_all[0, at], pt_all[1, at]], axis=0)
            return dot(weights, block, 1, 0, HI)

        two = jnp.concatenate([decompressed(zb), decompressed(zb + 1)], axis=1)
        update_ref[:, pl.ds(pl.multiple_of(i * 2 * rows, 2 * rows), 2 * rows)] = two.astype(
            update_ref.dtype
        )
        return carry

    lax.fori_loop(0, blocks // 2, spread, 0)

    for r in rounds:
        r.drain()

    def drain_step(q, carry):
        zb = place_of(q)

        @pl.when(inside(zb))
        def _():
            yp_copy(y, zb, q).wait_send()
            ym_copy(y, zb, q).wait_send()
            rp_copy(y_down, zb, q).wait_send()
            rm_copy(y_up, zb, q).wait_send()

        return carry

    lax.fori_loop(0, last, drain_step, 0)
    for q, to in ((1, z + 1), (2, z - 1)):

        @pl.when(inside(to))
        def _():
            z_copy(z, q, to).wait_send()

    def z_drain(q, carry):
        to = z + 2 * (q % 2) - 1

        @pl.when(jnp.logical_and(inside(place_of(q)), inside(to)))
        def _():
            z_copy(place_of(q), q + 2, to).wait_send()

        return carry

    lax.fori_loop(1, last, z_drain, 0)


def body(ny, nz, nh, activations, out_grads, error_buffer, right_factor):
    replicas = lax.axis_size("rep")
    ng = replicas // nh
    blocks = ny * nz
    _, rows, depth = activations.shape
    _, tok, width = out_grads.shape
    rank = right_factor.shape[0]
    r8, wy, zq = rank // ng, width // ny, nz // 2
    dma = lambda n: pltpu.SemaphoreType.DMA((n,))
    vm = lambda *s: pltpu.VMEM(s, F32)
    update, new_error, new_factor = pl.pallas_call(
        functools.partial(kernel, ny, nz, nh, replicas),
        out_shape=(
            jax.ShapeDtypeStruct((width // replicas, blocks * rows), jnp.bfloat16),
            jax.ShapeDtypeStruct((rows, width), F32),
            jax.ShapeDtypeStruct((rank, width), F32),
        ),
        in_specs=[pl.BlockSpec(memory_space=pltpu.VMEM)] * 4,
        out_specs=[pl.BlockSpec(memory_space=pltpu.VMEM)] * 3,
        scratch_shapes=[
            pltpu.VMEM((blocks, tok, width), jnp.bfloat16),
            vm(rows, width),
            vm(ng, rows // ng, rank),
            vm(ng, rows // ng, rank),
            vm(nh, rows // ng, rank),
            vm(ng, rows // ng, rank),
            vm(2, blocks, rank // 2, rows),
            vm(ny, r8, rank),
            vm(zq, r8, rank),
            vm(2, r8, rank),
            vm(ng, r8, rank),
            vm(ng, r8, width),
            vm(ng, r8, width),
            vm(ny, r8, wy),
            vm(ny, r8, wy),
            vm(zq, r8, wy),
            vm(2 * nh, r8, wy),
            vm(ny, r8, wy),
            vm(ng, r8, width),
        ]
        + [dma(2 * nz + 2)] * 10
        + [dma(80)] * 2,
        compiler_params=pltpu.CompilerParams(
            collective_id=0, has_side_effects=True, vmem_limit_bytes=40 * 2**20
        ),
    )(activations[0], out_grads[0], error_buffer[0], right_factor)
    return (update, new_error[None], new_factor)


def solution(mesh, ny=4, nh=2):
    nz = mesh.shape["outer"] // ny
    placed = (P("rep", "outer", None), P("rep", "outer", None), P("rep", "outer", None), P())
    return jax.shard_map(
        functools.partial(body, ny, nz, nh),
        mesh=mesh,
        in_specs=placed,
        out_specs=(P("rep", None), P("rep", "outer", None), P()),
        check_vma=False,
    )
```

time: 1230 us -> 156 us (0.13)
  waiting for transfers between devices: 731 us -> 0 us
  blocking collectives: 450 us -> 0 us
  Pallas kernels: 0 us -> 149 us
  other arithmetic: 14.6 us -> 0 us
  between operations: 14.8 us -> 0.65 us
    psum x1 -> x0, waiting for transfers between devices: 485 us -> none  [body(): new_factor = lax.psum(right_part, ('outer', 'rep')) / replicas]
    psum x2 -> x0, blocking collectives: 334 us -> none  [the longest x1 205 us: body(): gram = lax.psum(gram_part, 'outer')]
    all_gather x1 -> x0, waiting for transfers between devices: 246 us -> none  [body(): lax.all_gather(cotangents, 'outer', axis=0, tiled=True)]
    pallas_call x0 -> x1, Pallas kernels: none -> 149 us  [body(): pl.pallas_call(functools.partial(kernel, ny, nz, nh, replicas), out_shape...]
    all_gather x1 -> x0, blocking collectives: 115 us -> none  [body(): update = lax.all_gather(own_block, 'outer', axis=1, tiled=True)]
  transfers between devices with their start and end apart: 2 -> 0, of which waited for: 2 -> 0; matrix products, arithmetic and copies ran while one was open for 0% -> 0% of each run, Pallas kernels for 0% -> 0%
where the time goes in v1:
time: 156 us
  Pallas kernels  149 us (96%)
  local copies, waits for them, and re-layouts  6.9 us (4%)
    pallas_call x1, Pallas kernels, body(): pl.pallas_call(functools.partial(kernel, ny, nz, nh, replicas), out_shape...  149 us
    unnamed x11, local copies, waits for them, and re-layouts  6.9 us

profile of v1, /device:TPU:1, one launch (start us, length us, event | category | flops | bytes accessed | tf_op | source)
XLA Modules:
  0.0 156.2 jit_solution(1517060644839068680)
XLA Ops:
  0.6 0.0 copy-start
  0.6 1.4 copy-done
  2.0 0.0 copy-start.1
  2.0 1.1 copy-done.1
  3.2 0.0 copy-start.2
  3.2 0.9 copy-done.2
  4.1 0.0 copy-start.3
  4.1 0.9 copy-done.3
  5.1 148.7 %shard_map.67 = (bf16[64,6144]{1,0:T(8,128)(2,1)S(1)}, f32[192,1024]{1,0:T(8,128)S(1)}, f32[64,1024]{1,0:T(8,128)S(1)}) custom-call(bf16[192,4096]{1,0:T(8,128)(2,1)S(1)} %bitcast.4, bf16[128,1024]{1,0:T(8,128)(2,1)S(1)} %bitcast.7, f32[192,1024]{1,0:T(8,128)S(1)} %bitcast.6, f32[64,1024]{1,0:T(8,128)S(1)} %copy-done.3), custom_call_target="tpu_custom_call" | custom-call | tf_op jit(solution)/shard_map/pallas_call | solution.py:399
  153.8 0.9 copy.10
  154.6 0.9 copy.11
  155.5 0.7 copy.12
Async XLA Ops:
  0.6 1.4 copy-start
  2.0 1.1 copy-start.1
  3.2 0.9 copy-start.2
  4.1 0.9 copy-start.3

commit v2 on v1

v2 whole, which is shorter than its diff:
```python
import functools

import jax
import jax.numpy as jnp
from jax import lax
from jax.experimental import pallas as pl
from jax.experimental.pallas import tpu as pltpu
from jax.sharding import PartitionSpec as P

ZROWS = 0
HI = lax.Precision.HIGHEST
F32 = jnp.float32


def dot(a, b, ca, cb, precision=None):
    return lax.dot_general(
        a, b, (((ca,), (cb,)), ((), ())), precision=precision, preferred_element_type=F32
    )


def copy_to(src, dst, send, recv, outer, rep):
    return pltpu.make_async_remote_copy(
        src_ref=src,
        dst_ref=dst,
        send_sem=send,
        recv_sem=recv,
        device_id={"outer": outer, "rep": rep},
        device_id_type=pl.DeviceIdType.MESH,
    )


def parts(x):
    hi = x.astype(jnp.bfloat16)
    return hi, (x - hi.astype(F32)).astype(jnp.bfloat16)


class Round:
    def __init__(self, n, me, place, src, dst, send, recv, first):
        def out(k):
            to = lax.rem(me + k, n)
            return copy_to(src(to), dst(me), send.at[first + k - 1], recv.at[first + k - 1], *place(to))

        def into(k):
            to, frm = lax.rem(me + k, n), lax.rem(me + n - k, n)
            return copy_to(src(to), dst(frm), send.at[first + k - 1], recv.at[first + k - 1], *place(to))

        self.n, self.out, self.into = n, out, into

    def each(self, act):
        if self.n <= 8:
            for k in range(1, self.n):
                act(k)
        else:
            lax.fori_loop(1, self.n, lambda k, carry: (act(k), carry)[1], 0)

    def start(self):
        self.each(lambda k: self.out(k).start())

    def wait(self):
        self.each(lambda k: self.into(k).wait_recv())

    def drain(self):
        self.each(lambda k: self.out(k).wait_send())


def kernel(
    ny, nz, nh, replicas,
    a_ref, g_ref, e_ref, r_ref,
    update_ref, error_ref, factor_ref,
    g_all, a_in, r_in, corr, p_part, p_rs, p_h, p_all8,
    pt_all, gram_y, gram_z, gram_all,
    m_part, m_rs, m_z1, m_z2, m_all, spread_src, load_sem,
    z_send, z_recv, zf_send, zf_recv, yp_send, yp_recv, ym_send, ym_recv,
    rp_send, rp_recv, rm_send, rm_recv, send, recv,
):
    ng = replicas // nh
    zq = nz // 2
    blocks = ny * nz
    tok, width = g_ref.shape
    rank = r_ref.shape[0]
    rows = a_ref.shape[0]
    outer, rep = lax.axis_index("outer"), lax.axis_index("rep")
    y, z = outer // nz, outer % nz
    h, g = rep // ng, rep % ng
    core = rep % 2
    zlow, zhalf = z % zq, z // zq
    y_up, y_down, y_far = (y + 1) % ny, (y + ny - 1) % ny, (y + 2) % ny
    h_other = (h + 1) % nh

    barrier = pltpu.get_barrier_semaphore()
    unit = g * ny + y
    at_unit = lambda j: (j % ny * nz + z, h * ng + j // ny)
    peers = [at_unit((unit + k) % (ng * ny)) for k in range(1, ng * ny)]
    peers += [(y * nz + (z + k) % nz, rep) for k in range(1, nz)]
    peers += [(outer, h_other * ng + g), (y * nz + (z + zq) % nz, h_other * ng + g)]
    for o, r in peers:
        pl.semaphore_signal(
            barrier, inc=1, device_id={"outer": o, "rep": r},
            device_id_type=pl.DeviceIdType.MESH,
        )
    loads = [
        pltpu.make_async_copy(src, dst, load_sem.at[i])
        for i, (src, dst) in enumerate(
            ((g_ref, g_all.at[outer]), (e_ref, corr), (a_ref, a_in), (r_ref, r_in))
        )
    ]
    for c in loads:
        c.start()
    loads[0].wait()
    pl.semaphore_wait(barrier, len(peers))

    half = tok // 2
    step_n = min(256, width)

    def multiply(block):
        a = a_in[:, pl.ds(pl.multiple_of(block * tok, tok), tok)]
        for n in range(0, width, step_n):
            corr[:, n : n + step_n] += dot(a, g_all[block, :, n : n + step_n], 1, 0)

    def place_of(q):
        d = (q + 1) // 2
        return z + d * (1 - 2 * (q % 2))

    def z_copy(zb, q, to):
        slot = g_all.at[y * nz + zb]
        return copy_to(slot, slot, z_send.at[q], z_recv.at[q], y * nz + to, rep)

    def yp_copy(yb, zb, q):
        slot = g_all.at[yb * nz + zb]
        return copy_to(slot, slot, yp_send.at[q], yp_recv.at[q], y_up * nz + z, rep)

    def ym_copy(yb, zb, q):
        slot = g_all.at[yb * nz + zb]
        return copy_to(slot, slot, ym_send.at[q], ym_recv.at[q], y_down * nz + z, rep)

    relayed = half - ZROWS // 2

    def rp_copy(yb, zb, q, n=relayed):
        slot = g_all.at[yb * nz + zb, pl.ds(0, n)]
        return copy_to(slot, slot, rp_send.at[q], rp_recv.at[q], y_up * nz + z, rep)

    def rm_copy(yb, zb, q, n=relayed):
        slot = g_all.at[yb * nz + zb, pl.ds(n, n)]
        return copy_to(slot, slot, rm_send.at[q], rm_recv.at[q], y_down * nz + z, rep)

    def zf_copy(zb, q, to):
        slot = g_all.at[y_far * nz + zb, pl.ds(tok - ZROWS, ZROWS)]
        return copy_to(slot, slot, zf_send.at[q], zf_recv.at[q], y * nz + to, rep)

    def inside(zb):
        return jnp.logical_and(zb >= 0, zb < nz)

    for q, to in ((1, z + 1), (2, z - 1)):

        @pl.when(inside(to))
        def _():
            z_copy(z, q, to).start()

    yp_copy(y, z, 0).start()
    ym_copy(y, z, 0).start()
    for c in loads[1:]:
        c.wait()
    multiply(outer)
    last = 2 * nz - 1

    def z_step(q, send_y=True):
        zb = place_of(q)

        @pl.when(inside(zb))
        def _():
            z_copy(zb, q, (z + 1) % nz).wait_recv()
            to = z + 2 * (q % 2) - 1

            @pl.when(inside(to))
            def _():
                z_copy(zb, q + 2, to).start()

            if send_y:
                z_sent(q)

    def z_sent(q):
        zb = place_of(q)
        yp_copy(y, zb, q).start()
        ym_copy(y, zb, q).start()
        multiply(y * nz + zb)

    def y_step(q, n):
        zb = place_of(q)
        yp_copy(y_down, zb, q).wait_recv()
        rp_copy(y_down, zb, q, n).start()
        ym_copy(y_up, zb, q).wait_recv()
        rm_copy(y_up, zb, q, n).start()

    def y_multiply(q):
        zb = place_of(q)
        multiply(y_down * nz + zb)
        multiply(y_up * nz + zb)

    def far_step(q, n):
        zb = place_of(q)
        rp_copy(y_far, zb, q, n).wait_recv()
        rm_copy(y_far, zb, q, n).wait_recv()
        multiply(y_far * nz + zb)

    def zf_step(q):
        zb = place_of(q)
        zf_copy(zb, q, (z + 1) % nz).wait_recv()
        to = z + 2 * (q % 2) - 1

        @pl.when(inside(to))
        def _():
            zf_copy(zb, q + 2, to).start()

    def loop(lo, hi, step):
        def guarded(q, carry):
            @pl.when(inside(place_of(q)))
            def _():
                step(q)

            return carry

        lax.fori_loop(lo, hi, guarded, 0)

    if ZROWS:
        loop(1, 3, lambda q: z_step(q, False))
        y_step(0, half)
        loop(1, 3, z_sent)
        y_multiply(0)
        loop(3, last, z_step)
        far_step(0, half)
        for q, to in ((1, z + 1), (2, z - 1)):

            @pl.when(inside(to))
            def _():
                zf_copy(z, q, to).start()

        def both(q):
            y_step(q, relayed)
            zf_step(q)
            y_multiply(q)

        loop(1, last, both)
    else:
        loop(1, last, z_step)
        y_step(0, half)
        y_multiply(0)

        def relay(q):
            y_step(q, relayed)
            y_multiply(q)

        loop(1, last, relay)
        far_step(0, half)
    loop(1, last, lambda q: far_step(q, relayed))

    rows8 = rows // ng
    part = dot(corr[...], r_in[...], 1, 1, HI) * (1.0 / replicas)
    p_part[...] = part.reshape(ng, rows8, rank)
    group = lambda j: (outer, h * ng + j)
    count = [0]

    def make(n, me, place, src, dst):
        first = count[0]
        count[0] += n - 1
        return Round(n, me, place, src, dst, send, recv, first)

    rounds = []

    def go(*args):
        r = make(*args)
        rounds.append(r)
        r.start()
        return r

    def total(ref, n):
        s = ref[0]
        for i in range(1, n):
            s = s + ref[i]
        return s

    rnd = go(ng, g, group, lambda j: p_part.at[j], lambda i: p_rs.at[i])
    p_rs[g] = p_part[g]
    rnd.wait()
    p_h[h] = total(p_rs, ng)
    if nh > 1:
        rnd = go(nh, h, lambda j: (outer, j * ng + g), lambda j: p_h.at[h], lambda i: p_h.at[i])
        rnd.wait()
    p_all8[g] = total(p_h, nh)
    rnd = go(ng, g, group, lambda j: p_all8.at[g], lambda i: p_all8.at[i])
    rnd.wait()
    p = p_all8[...].reshape(rows, rank)

    r8 = rank // ng
    pt = p.T
    gram_all[...] = dot(pt, pt, 1, 1, HI).reshape(ng, r8, rank)
    gram_y[y] = gram_all[g]
    in_y = lambda j: (j * nz + z, rep)
    in_z1 = lambda j: (y * nz + zhalf * zq + j, rep)
    gram_1 = go(ny, y, in_y, lambda j: gram_y.at[y], lambda i: gram_y.at[i])

    hr = rank // 2
    slot = y * nz + zlow * 2 + zhalf
    piece = jnp.where(core == 0, pt[:hr], pt[hr:])
    lanes = 128
    tail = piece[:, lanes:]
    pt_all[core, slot, :hr] = piece[:, :lanes]
    pt_all[core, slot, hr:] = jnp.concatenate([tail[: hr // 2], tail[hr // 2 :]], axis=1)
    pt_1 = go(
        2, zhalf, lambda j: (y * nz + j * zq + zlow, rep),
        lambda j: pt_all.at[core, slot],
        lambda i: pt_all.at[core, y * nz + zlow * 2 + i],
    )

    wy = width // ny
    for i in range(ny):
        chunk = dot(pt, corr[:, i * wy : (i + 1) * wy], 1, 0, HI)
        m_part[:, i] = chunk.reshape(ng, r8, wy)
    m_1 = go(
        ng * ny, unit, at_unit, lambda j: m_part.at[j // ny, j % ny], lambda i: m_rs.at[i]
    )
    m_rs[unit] = m_part[g, y]

    gram_1.wait()
    gram_z[z] = total(gram_y, ny)
    gram_2 = go(
        nz, z, lambda j: (y * nz + j, rep), lambda j: gram_z.at[z], lambda i: gram_z.at[i]
    )
    pt_1.wait()
    pair = lambda i: pt_all.at[core, pl.ds(y * nz + i * 2, 2)]
    pt_2 = go(zq, zlow, in_z1, lambda j: pair(zlow), pair)

    m_1.wait()
    m_z1[zlow] = total(m_rs, ng * ny)
    m_3 = go(zq, zlow, in_z1, lambda j: m_z1.at[zlow], lambda i: m_z1.at[i])

    pt_2.wait()
    column = lambda i: pt_all.at[core, pl.ds(i * nz, nz)]
    pt_3 = go(ny, y, in_y, lambda j: column(y), column)
    gram_2.wait()
    gram_all[g] = total(gram_z, nz)
    gram_4 = go(ng, g, group, lambda j: gram_all.at[g], lambda i: gram_all.at[i])
    m_3.wait()
    w = h * 2 + zhalf
    m_z2[w] = total(m_z1, zq)
    m_4 = go(
        2 * nh, w, lambda j: (y * nz + j % 2 * zq + zlow, j // 2 * ng + g),
        lambda j: m_z2.at[w], lambda i: m_z2.at[i],
    )

    gram_4.wait()
    gram = gram_all[...].reshape(rank, rank)
    ri = lax.broadcasted_iota(jnp.int32, (rank, rank), 0)
    ci = lax.broadcasted_iota(jnp.int32, (rank, rank), 1)
    eye = (ri == ci).astype(F32)
    gram = gram + (0.0001 / rank) * jnp.sum(gram * eye) * eye
    full = jnp.concatenate([gram, eye], axis=1)
    x = [full[i : i + 8] for i in range(0, rank, 8)]
    sub = lax.broadcasted_iota(jnp.int32, (8, 1), 0)

    def eliminate(x, lo, hi):
        x = list(x)
        for j in range(lo, hi):
            b, i = divmod(j, 8)
            row = x[b][i : i + 1]
            scaled = row / row[:, j : j + 1]
            for k in range(b, len(x)):
                col = x[k][:, j : j + 1]
                if k == b:
                    col = jnp.where(sub > i, col, 0.0)
                x[k] = x[k] - col * scaled
        return x

    x = eliminate(x, 0, rank)
    m_4.wait()
    m_all[g, y] = total(m_z2, 2 * nh) * (1.0 / replicas)
    in_all = lambda i: m_all.at[i // ny, i % ny]
    m_6 = go(ng * ny, unit, at_unit, lambda j: m_all.at[g, y], in_all)
    pt_3.wait()
    side = lambda i: pt_all.at[i]
    pt_4 = go(2, core, lambda j: (outer, rep // 2 * 2 + j), lambda j: side(core), side)

    full = jnp.concatenate(x, axis=0)
    pivots = jnp.sum(full[:, :rank] * eye, axis=1, keepdims=True)
    inverse = full[:, rank:] * (1.0 / jnp.sqrt(pivots))
    hi, mid = parts(dot(p, inverse, 1, 1, HI))
    p_orth = jnp.concatenate([hi, hi, mid, mid], axis=1)
    for r in rounds[:-2]:
        r.drain()
    for k in (yp_copy, ym_copy):
        k(y, z, 0).wait_send()
    rp_copy(y_down, z, 0, half).wait_send()
    rm_copy(y_up, z, 0, half).wait_send()

    def drain(q):
        zb = place_of(q)
        yp_copy(y, zb, q).wait_send()
        ym_copy(y, zb, q).wait_send()
        rp_copy(y_down, zb, q).wait_send()
        rm_copy(y_up, zb, q).wait_send()
        to = z + 2 * (q % 2) - 1

        @pl.when(inside(to))
        def _():
            z_copy(zb, q + 2, to).wait_send()
            if ZROWS:
                zf_copy(zb, q + 2, to).wait_send()

    loop(1, last, drain)
    for q, to in ((1, z + 1), (2, z - 1)):

        @pl.when(inside(to))
        def _():
            z_copy(z, q, to).wait_send()
            if ZROWS:
                zf_copy(z, q, to).wait_send()

    pt_4.wait()

    def orthogonal(i, carry):
        yb, zb = i // (nz // 2), i % (nz // 2) * 2

        def block(zb):
            at = yb * nz + zb % zq * 2 + zb // zq
            head = jnp.concatenate([pt_all[0, at, :hr], pt_all[1, at, :hr]], axis=0)
            t0, t1 = pt_all[0, at, hr:], pt_all[1, at, hr:]
            w = rows - lanes
            tail = jnp.concatenate([t0[:, :w], t0[:, w:], t1[:, :w], t1[:, w:]], axis=0)
            return jnp.concatenate([head, tail], axis=1)

        two = jnp.concatenate([block(zb), block(zb + 1)], axis=1)
        hi, mid = parts(dot(inverse, two, 1, 0, HI))
        spread_src[i] = jnp.concatenate([hi, mid, hi, mid], axis=0)
        return carry

    lax.fori_loop(0, blocks // 2, orthogonal, 0, unroll=2)

    m_6.wait()
    for i in range(ny):
        cut = slice(i * wy, (i + 1) * wy)
        factor = dot(inverse, m_all[:, i].reshape(rank, wy), 1, 0, HI)
        factor_ref[:, cut] = factor
        hi, mid = parts(factor)
        factor = jnp.concatenate([hi, mid, hi, mid], axis=0)
        error_ref[:, cut] = corr[:, cut] - dot(p_orth, factor, 1, 0)
    columns = width // replicas
    both = factor_ref[:, pl.ds(pl.multiple_of(rep // 2 * (2 * columns), 2 * columns), 2 * columns)]
    hi, mid = parts(jnp.where(core == 0, both[:, :columns], both[:, columns:]))
    own = jnp.concatenate([hi, hi, mid, mid], axis=0)

    def spread(i, carry):
        update_ref[:, pl.ds(pl.multiple_of(i * 2 * rows, 2 * rows), 2 * rows)] = dot(
            own, spread_src[i], 0, 0
        ).astype(update_ref.dtype)
        return carry

    lax.fori_loop(0, blocks // 2, spread, 0, unroll=4)

    pt_4.drain()
    m_6.drain()


def body(ny, nz, nh, activations, out_grads, error_buffer, right_factor):
    replicas = lax.axis_size("rep")
    ng = replicas // nh
    blocks = ny * nz
    _, rows, depth = activations.shape
    _, tok, width = out_grads.shape
    rank = right_factor.shape[0]
    r8, wy, zq = rank // ng, width // ny, nz // 2
    dma = lambda n: pltpu.SemaphoreType.DMA((n,))
    vm = lambda *s: pltpu.VMEM(s, F32)
    update, new_error, new_factor = pl.pallas_call(
        functools.partial(kernel, ny, nz, nh, replicas),
        out_shape=(
            jax.ShapeDtypeStruct((width // replicas, blocks * rows), jnp.bfloat16),
            jax.ShapeDtypeStruct((rows, width), F32),
            jax.ShapeDtypeStruct((rank, width), F32),
        ),
        in_specs=[pl.BlockSpec(memory_space=pltpu.HBM)] * 4,
        out_specs=[pl.BlockSpec(memory_space=pltpu.VMEM)] * 3,
        scratch_shapes=[
            pltpu.VMEM((blocks, tok, width), jnp.bfloat16),
            pltpu.VMEM((rows, depth), jnp.bfloat16),
            vm(rank, width),
            vm(rows, width),
            vm(ng, rows // ng, rank),
            vm(ng, rows // ng, rank),
            vm(nh, rows // ng, rank),
            vm(ng, rows // ng, rank),
            vm(2, blocks, rank // 2 * rows // 128, 128),
            vm(ny, r8, rank),
            vm(nz, r8, rank),
            vm(ng, r8, rank),
            vm(ng, ny, r8, wy),
            vm(ng * ny, r8, wy),
            vm(zq, r8, wy),
            vm(2 * nh, r8, wy),
            vm(ng, ny, r8, wy),
            pltpu.VMEM((blocks // 2, 4 * rank, 2 * rows), jnp.bfloat16),
            dma(4),
        ]
        + [dma(2 * nz + 2)] * 12
        + [dma(112)] * 2,
        compiler_params=pltpu.CompilerParams(
            collective_id=0, has_side_effects=True, vmem_limit_bytes=63 * 2**20
        ),
    )(activations[0], out_grads[0], error_buffer[0], right_factor)
    return (update, new_error[None], new_factor)


def solution(mesh, ny=4, nh=2):
    nz = mesh.shape["outer"] // ny
    placed = (P("rep", "outer", None), P("rep", "outer", None), P("rep", "outer", None), P())
    return jax.shard_map(
        functools.partial(body, ny, nz, nh),
        mesh=mesh,
        in_specs=placed,
        out_specs=(P("rep", None), P("rep", "outer", None), P()),
        check_vma=False,
    )
```

time: 156 us -> 145 us (0.929)
  Pallas kernels: 149 us -> 140 us
  local copies, waits for them, and re-layouts: 6.9 us -> 3.74 us
    pallas_call x1, Pallas kernels: 149 us -> 140 us  [body(): pl.pallas_call(functools.partial(kernel, ny, nz, nh, replicas), out_shape...]
    unnamed x11 -> x7, local copies, waits for them, and re-layouts: 6.9 us -> 3.74 us
where the time goes in v2:
time: 145 us
  Pallas kernels  140 us (97%)
  local copies, waits for them, and re-layouts  3.74 us (3%)
    pallas_call x1, Pallas kernels, body(): pl.pallas_call(functools.partial(kernel, ny, nz, nh, replicas), out_shape...  140 us
    unnamed x7, local copies, waits for them, and re-layouts  3.74 us

profile of v2, /device:TPU:1, one launch (start us, length us, event | category | flops | bytes accessed | tf_op | source)
XLA Modules:
  0.0 144.8 jit_solution(15417121865207116274)
XLA Ops:
  0.6 140.4 %shard_map.67 = (bf16[64,6144]{1,0:T(8,128)(2,1)}, f32[192,1024]{1,0:T(8,128)}, f32[64,1024]{1,0:T(8,128)}) custom-call(bf16[192,4096]{1,0:T(8,128)(2,1)} %bitcast.4, bf16[128,1024]{1,0:T(8,128)(2,1)} %bitcast.7, f32[192,1024]{1,0:T(8,128)} %bitcast.6, f32[64,1024]{1,0:T(8,128)} %r_ref.1), custom_call_target="tpu_custom_call" | custom-call | tf_op jit(solution)/shard_map/pallas_call | solution.py:472
  141.0 0.0 copy-start
  141.0 0.0 copy-start.1
  141.0 2.1 %copy.10 = bf16[64,6144]{1,0:T(8,128)(2,1)} copy(bf16[64,6144]{1,0:T(8,128)(2,1)} %get-tuple-element.12) | data formatting | bytes 1572864
  143.2 0.0 copy-done
  143.2 0.9 copy.11
  144.1 0.0 copy-done.1
  144.1 0.7 copy.12
Async XLA Ops:
  141.0 2.2 %copy-start = (f32[192,1024]{1,0:T(8,128)S(1)}, f32[192,1024]{1,0:T(8,128)}, u32[]{:S(2)}) copy-start(f32[192,1024]{1,0:T(8,128)} %get-tuple-element.7) | copy-start | bytes 2359300
  141.0 3.0 %copy-start.1 = (f32[64,1024]{1,0:T(8,128)S(1)}, f32[64,1024]{1,0:T(8,128)}, u32[]{:S(2)}) copy-start(f32[64,1024]{1,0:T(8,128)} %get-tuple-element.14) | copy-start | bytes 786436

commit v3 on v2

--- a/solution.py
+++ b/solution.py
@@ -7,7 +7,7 @@
 from jax.experimental.pallas import tpu as pltpu
 from jax.sharding import PartitionSpec as P
 
-ZROWS = 0
+ZROWS = 32
 HI = lax.Precision.HIGHEST
 F32 = jnp.float32
 
@@ -222,9 +222,8 @@
         lax.fori_loop(lo, hi, guarded, 0)
 
     if ZROWS:
-        loop(1, 3, lambda q: z_step(q, False))
+        loop(1, 3, z_step)
         y_step(0, half)
-        loop(1, 3, z_sent)
         y_multiply(0)
         loop(3, last, z_step)
         far_step(0, half)
@@ -236,8 +235,8 @@
 
         def both(q):
             y_step(q, relayed)
+            y_multiply(q)
             zf_step(q)
-            y_multiply(q)
 
         loop(1, last, both)
     else:

time: 145 us -> 143 us (0.986)
  Pallas kernels: 140 us -> 138 us
    pallas_call x1, Pallas kernels: 140 us -> 138 us  [body(): pl.pallas_call(functools.partial(kernel, ny, nz, nh, replicas), out_shape...]
where the time goes in v3:
time: 143 us
  Pallas kernels  138 us (97%)
  local copies, waits for them, and re-layouts  3.74 us (3%)
    pallas_call x1, Pallas kernels, body(): pl.pallas_call(functools.partial(kernel, ny, nz, nh, replicas), out_shape...  138 us
    unnamed x7, local copies, waits for them, and re-layouts  3.74 us

profile of v3, /device:TPU:1, one launch (start us, length us, event | category | flops | bytes accessed | tf_op | source)
XLA Modules:
  0.0 142.8 jit_solution(10556593843527284910)
XLA Ops:
  0.6 138.4 %shard_map.67 = (bf16[64,6144]{1,0:T(8,128)(2,1)}, f32[192,1024]{1,0:T(8,128)}, f32[64,1024]{1,0:T(8,128)}) custom-call(bf16[192,4096]{1,0:T(8,128)(2,1)} %bitcast.4, bf16[128,1024]{1,0:T(8,128)(2,1)} %bitcast.7, f32[192,1024]{1,0:T(8,128)} %bitcast.6, f32[64,1024]{1,0:T(8,128)} %r_ref.1), custom_call_target="tpu_custom_call" | custom-call | tf_op jit(solution)/shard_map/pallas_call | solution.py:471
  139.0 0.0 copy-start
  139.1 0.0 copy-start.1
  139.1 2.1 %copy.10 = bf16[64,6144]{1,0:T(8,128)(2,1)} copy(bf16[64,6144]{1,0:T(8,128)(2,1)} %get-tuple-element.12) | data formatting | bytes 1572864
  141.2 0.0 copy-done
  141.2 0.9 copy.11
  142.1 0.0 copy-done.1
  142.1 0.7 copy.12
Async XLA Ops:
  139.0 2.2 %copy-start = (f32[192,1024]{1,0:T(8,128)S(1)}, f32[192,1024]{1,0:T(8,128)}, u32[]{:S(2)}) copy-start(f32[192,1024]{1,0:T(8,128)} %get-tuple-element.7) | copy-start | bytes 2359300
  139.1 3.0 %copy-start.1 = (f32[64,1024]{1,0:T(8,128)S(1)}, f32[64,1024]{1,0:T(8,128)}, u32[]{:S(2)}) copy-start(f32[64,1024]{1,0:T(8,128)} %get-tuple-element.14) | copy-start | bytes 786436

commit v4 on v3

--- a/solution.py
+++ b/solution.py
@@ -369,7 +369,8 @@
                 x[k] = x[k] - col * scaled
         return x
 
-    x = eliminate(x, 0, rank)
+    most = rank * 5 // 8
+    x = eliminate(x, 0, most)
     m_4.wait()
     m_all[g, y] = total(m_z2, 2 * nh) * (1.0 / replicas)
     in_all = lambda i: m_all.at[i // ny, i % ny]
@@ -378,6 +379,7 @@
     side = lambda i: pt_all.at[i]
     pt_4 = go(2, core, lambda j: (outer, rep // 2 * 2 + j), lambda j: side(core), side)
 
+    x = eliminate(x, most, rank)
     full = jnp.concatenate(x, axis=0)
     pivots = jnp.sum(full[:, :rank] * eye, axis=1, keepdims=True)
     inverse = full[:, rank:] * (1.0 / jnp.sqrt(pivots))

time: 143 us -> 145 us (1.014)
  Pallas kernels: 138 us -> 140 us
    pallas_call x1, Pallas kernels: 138 us -> 140 us  [body(): pl.pallas_call(functools.partial(kernel, ny, nz, nh, replicas), out_shape...]
where the time goes in v4:
time: 145 us; the launch traced here: 144 us
  Pallas kernels  140 us (97%)
  local copies, waits for them, and re-layouts  3.74 us (3%)
    pallas_call x1, Pallas kernels, body(): pl.pallas_call(functools.partial(kernel, ny, nz, nh, replicas), out_shape...  140 us
    unnamed x7, local copies, waits for them, and re-layouts  3.74 us

profile of v4, /device:TPU:1, one launch (start us, length us, event | category | flops | bytes accessed | tf_op | source)
XLA Modules:
  0.0 144.4 jit_solution(18258437739283618403)
XLA Ops:
  0.6 140.0 %shard_map.67 = (bf16[64,6144]{1,0:T(8,128)(2,1)}, f32[192,1024]{1,0:T(8,128)}, f32[64,1024]{1,0:T(8,128)}) custom-call(bf16[192,4096]{1,0:T(8,128)(2,1)} %bitcast.4, bf16[128,1024]{1,0:T(8,128)(2,1)} %bitcast.7, f32[192,1024]{1,0:T(8,128)} %bitcast.6, f32[64,1024]{1,0:T(8,128)} %r_ref.1), custom_call_target="tpu_custom_call" | custom-call | tf_op jit(solution)/shard_map/pallas_call | solution.py:473
  140.6 0.0 copy-start
  140.6 0.0 copy-start.1
  140.6 2.1 %copy.10 = bf16[64,6144]{1,0:T(8,128)(2,1)} copy(bf16[64,6144]{1,0:T(8,128)(2,1)} %get-tuple-element.12) | data formatting | bytes 1572864
  142.8 0.0 copy-done
  142.8 0.9 copy.11
  143.7 0.0 copy-done.1
  143.7 0.7 copy.12
Async XLA Ops:
  140.6 2.2 %copy-start = (f32[192,1024]{1,0:T(8,128)S(1)}, f32[192,1024]{1,0:T(8,128)}, u32[]{:S(2)}) copy-start(f32[192,1024]{1,0:T(8,128)} %get-tuple-element.7) | copy-start | bytes 2359300
  140.6 3.0 %copy-start.1 = (f32[64,1024]{1,0:T(8,128)S(1)}, f32[64,1024]{1,0:T(8,128)}, u32[]{:S(2)}) copy-start(f32[64,1024]{1,0:T(8,128)} %get-tuple-element.14) | copy-start | bytes 786436
